TPU v7x, 32 devices: a whole 2x2x4 slice. The times are simulated.
32 devices in a mesh: groups: 2 (over x), expert: 16 (over z, y, core).
Axes of the slice: x: 2, y: 2, z: 4, core: 2. Of those that a mesh axis runs over, the one named last changes fastest.
Arguments:
- tokens: bfloat16 [4096, 2048], P(('groups', 'expert')), parts along dimension 0, may hold values from -6 to 6
- cotangent: bfloat16 [4096, 2048], P(('groups', 'expert')), parts along dimension 0, may hold values from -1.5 to 1.5
- expert_ids: int32 [4096, 3], P(('groups', 'expert')), parts along dimension 0, may hold values from 0 to 15, all different within a row; in each aligned block of 128 rows (0 to 127, 128 to 255, ...) at most 48 rows name the same one
- combine: float32 [4096, 3], P(('groups', 'expert')), parts along dimension 0, may hold values from 0.2 to 1
- w_gate: bfloat16 [16, 2048, 768], P('expert'), may hold values from -0.125 to 0.125
- w_up: bfloat16 [16, 2048, 768], P('expert'), may hold values from -0.125 to 0.125
- w_down: bfloat16 [16, 768, 2048], P('expert'), may hold values from -0.21875 to 0.21875
Outputs:
- mixed: bfloat16 [4096, 2048], P(('groups', 'expert')), parts along dimension 0
- grad_tokens: bfloat16 [4096, 2048], P(('groups', 'expert')), parts along dimension 0
- grad_combine: float32 [4096, 3], P(('groups', 'expert')), parts along dimension 0
There are 2 independent parts, one for each index of `groups`. A program takes and returns all parts, laid end to end along the dimension named above; an argument that names none is the same for every part. Nothing has to cross between parts.
Inputs may be any that keep to these rules, and one draw needn't show every extreme that they name: `expert_ids`: each token names 3 different experts. In the rows of one device (aligned blocks of 128 tokens) no expert is named more than 48 times, a bound that some block reaches.
All inputs are finite; a program needn't handle non-finite values.
Results may differ from a plain program's by a relative error of at most 0.008.
Values may be sent and summed in bfloat16 or wider, within the bound.
A program may use at most 128 MiB of HBM per device.

v0:
```python
import jax
import jax.numpy as jnp
from jax import lax
from jax.sharding import PartitionSpec as P


def expert_rows(row_inputs, row_grads, weights):
    w_gate, w_up, w_down = weights
    gate = jnp.dot(row_inputs, w_gate, preferred_element_type=jnp.float32)
    upper = jnp.dot(row_inputs, w_up, preferred_element_type=jnp.float32)
    sigmoid_gate = jax.nn.sigmoid(gate)
    activated = gate * sigmoid_gate
    hidden = (activated * upper).astype(jnp.bfloat16)
    output = jnp.dot(hidden, w_down, preferred_element_type=jnp.float32).astype(jnp.bfloat16)
    d_hidden = lax.dot_general(
        row_grads, w_down, (((1,), (1,)), ((), ())), preferred_element_type=jnp.float32
    )
    d_gate = (d_hidden * upper * sigmoid_gate * (1.0 + gate * (1.0 - sigmoid_gate))).astype(
        jnp.bfloat16
    )
    d_upper = (d_hidden * activated).astype(jnp.bfloat16)
    back_rows = lax.dot_general(
        d_gate, w_gate, (((1,), (1,)), ((), ())), preferred_element_type=jnp.float32
    )
    back_rows = back_rows + lax.dot_general(
        d_upper, w_up, (((1,), (1,)), ((), ())), preferred_element_type=jnp.float32
    )
    return (output, back_rows.astype(jnp.bfloat16))


def on_device(tokens, cotangent, expert_ids, combine, w_gate, w_up, w_down):
    holders = lax.axis_size("expert")
    tok_rows, model_width = tokens.shape
    fanout = expert_ids.shape[1]
    capacity = 2 * tok_rows * fanout // holders
    count_rows = tok_rows * fanout
    flat_ids = expert_ids.reshape(count_rows)
    onehot = (flat_ids[:, None] == jnp.arange(holders, dtype=jnp.int32)[None, :]).astype(jnp.int32)
    rank_in = jnp.sum((jnp.cumsum(onehot, axis=0) - onehot) * onehot, axis=1)
    own_weights = (w_gate[0], w_up[0], w_down[0])
    slot_flat = flat_ids * capacity + rank_in
    total_slots = holders * capacity
    row_of_slot = (
        jnp.full((total_slots,), count_rows, jnp.int32)
        .at[slot_flat]
        .set(jnp.arange(count_rows, dtype=jnp.int32))
    )
    filled = row_of_slot < count_rows
    token_of_slot = jnp.minimum(row_of_slot, count_rows - 1) // fanout
    send_x = jnp.where(filled[:, None], tokens[token_of_slot], 0).reshape(
        holders, capacity, model_width
    )
    send_g = jnp.where(filled[:, None], cotangent[token_of_slot], 0).reshape(
        holders, capacity, model_width
    )
    got_x, got_g = (
        lax.all_to_all(send_x, "expert", split_axis=0, concat_axis=0, tiled=True),
        lax.all_to_all(send_g, "expert", split_axis=0, concat_axis=0, tiled=True),
    )
    flat_out, flat_back = expert_rows(
        got_x.reshape(total_slots, model_width),
        got_g.reshape(total_slots, model_width),
        own_weights,
    )
    result_out = flat_out.reshape(holders, capacity, model_width)
    result_back = flat_back.reshape(holders, capacity, model_width)
    back_out, back_grad = (
        lax.all_to_all(result_out, "expert", split_axis=0, concat_axis=0, tiled=True),
        lax.all_to_all(result_back, "expert", split_axis=0, concat_axis=0, tiled=True),
    )
    out_rows = (
        back_out.reshape(total_slots, model_width)[slot_flat]
        .reshape(tok_rows, fanout, model_width)
        .astype(jnp.float32)
    )
    grad_rows = (
        back_grad.reshape(total_slots, model_width)[slot_flat]
        .reshape(tok_rows, fanout, model_width)
        .astype(jnp.float32)
    )
    mixed = jnp.einsum("tk,tkd->td", combine, out_rows).astype(jnp.bfloat16)
    grad_tokens = jnp.einsum("tk,tkd->td", combine, grad_rows).astype(jnp.bfloat16)
    grad_combine = jnp.einsum("td,tkd->tk", cotangent.astype(jnp.float32), out_rows)
    return (mixed, grad_tokens, grad_combine)


def solution(mesh):
    placed = (
        P(("groups", "expert"), None),
        P(("groups", "expert"), None),
        P(("groups", "expert"), None),
        P(("groups", "expert"), None),
        P("expert", None, None),
        P("expert", None, None),
        P("expert", None, None),
    )
    return jax.shard_map(
        on_device,
        mesh=mesh,
        in_specs=placed,
        out_specs=(
            P(("groups", "expert"), None),
            P(("groups", "expert"), None),
            P(("groups", "expert"), None),
        ),
        check_vma=False,
    )
```

profile of v0, /device:TPU:13, one launch (start us, length us, event | category | flops | bytes accessed | tf_op | source)
XLA Modules:
  0.0 346.6 jit_solution(12204052320452651692)
XLA Ops:
  0.6 0.0 copy-start
  0.6 0.8 broadcast_multiply_fusion
  1.5 0.9 copy.11
  2.4 0.2 eq.29
  2.6 0.2 eq.25
  2.8 0.1 copy.10
  2.9 0.2 mul.42
  3.1 0.9 reduce-window.6
  4.0 0.2 slice_reduce_fusion
  4.3 0.1 fusion.18
  4.4 2.9 scatter_custom_fusion
  7.4 0.1 broadcast_in_dim.28
  7.5 8.2 %gather_fusion.2 = bf16[768,2048]{1,0:T(8,128)(2,1)} fusion(bf16[128,2048]{1,0:T(8,128)(2,1)} %param.8, s32[1024]{0:T(1024)S(1)} %pad_clamp_fusion.1), kind=kCustom, calls=%fused_computation.2 | custom fusion | bytes 6294528 | tf_op jit(solution)/shard_map/gather | solution.py:53
  15.7 8.3 %gather_fusion = bf16[768,2048]{1,0:T(8,128)(2,1)} fusion(bf16[128,2048]{1,0:T(8,128)(2,1)} %param.7, s32[1024]{0:T(1024)S(1)} %pad_clamp_fusion.1), kind=kCustom, calls=%fused_computation | custom fusion | bytes 6294528 | tf_op jit(solution)/shard_map/gather | solution.py:50
  24.0 4.3 %broadcast_select_fusion = (bf16[16,48,2048]{2,1,0:T(8,128)(2,1)}, bf16[16,48,2048]{2,1,0:T(8,128)(2,1)S(1)}) fusion(bf16[16,48,2048]{2,1,0:T(8,128)(2,1)} %bitcast.60, pred[16,48]{1,0:T(8,128)(4,1)S(1)} %broadcast_in_dim.28, bf16[16,48,2048]{2,1,0:T(8,128)(2,1)} %bitcast.61), kind=kLoop, calls=%fused_computation.17 | loop fusion | flops 3145728 | bytes 12583680 | tf_op jit(solution)/shard_map/jit(_where)/select_n | solution.py:53
  28.3 76.2 %all_to_all.20 = bf16[16,48,2048]{2,1,0:T(8,128)(2,1)} all-to-all(bf16[16,48,2048]{2,1,0:T(8,128)(2,1)S(1)} %get-tuple-element.4), channel_id=1, replica_groups=mesh['groups'=2,'expert'=16] {'expert'}, dimensions={0} | all-to-all | bytes 6291456 | tf_op jit(solution)/shard_map/all_to_all | solution.py:57
  104.5 5.2 %all-to-all-start.2 = ((bf16[16,48,2048]{2,1,0:T(8,128)(2,1)}), bf16[16,48,2048]{2,1,0:T(8,128)(2,1)}, u32[]{:S(2)}, u32[]{:S(2)}) async-start(bf16[16,48,2048]{2,1,0:T(8,128)(2,1)} %get-tuple-element.3), calls=%async_computation.2 | async-start | bytes 6291456 | tf_op jit(solution)/shard_map/all_to_all | solution.py:58
  109.7 0.0 copy-start.5
  109.7 5.6 %fusion.8 = f32[768,768]{1,0:T(8,128)S(1)} fusion(bf16[768,2048]{1,0:T(8,128)(2,1)} %bitcast.64, bf16[1,2048,768]{2,1,0:T(8,128)(2,1)} %param.11), kind=kOutput, calls=%fused_computation.15 | convolution fusion | flops 2415919104 | bytes 8650752 | tf_op jit(solution)/shard_map/dot_general | solution.py:9
  115.3 0.0 copy-done.1
  115.3 0.0 copy-done.5
  115.3 0.0 copy-start.7
  115.3 2.6 fusion.4
  117.9 0.0 copy-done.7
  117.9 0.0 copy-start.9
  117.9 1.4 copy-done.9
  119.3 0.0 copy-done
  119.3 4.0 %convolution_convert_fusion = bf16[768,2048]{1,0:T(8,128)(2,1)} fusion(bf16[1,768,2048]{2,1,0:T(8,128)(2,1)S(1)} %copy-done, f32[768,768]{1,0:T(8,128)S(1)} %fusion.4, f32[768,768]{1,0:T(8,128)S(1)} %fusion.8), kind=kOutput, calls=%fused_computation.6 | convolution fusion | flops 2421030912 | bytes 11010048 | tf_op jit(solution)/shard_map/dot_general | solution.py:14
  123.4 56.3 %all-to-all-done.2 = bf16[16,48,2048]{2,1,0:T(8,128)(2,1)} async-done(((bf16[16,48,2048]{2,1,0:T(8,128)(2,1)}), bf16[16,48,2048]{2,1,0:T(8,128)(2,1)}, u32[]{:S(2)}, u32[]{:S(2)}) %all-to-all-start.2) | async-done | bytes 3145760 | tf_op jit(solution)/shard_map/all_to_all | solution.py:58
  179.7 4.9 %all-to-all-start.1 = ((bf16[16,48,2048]{2,1,0:T(8,128)(2,1)}), bf16[16,48,2048]{2,1,0:T(8,128)(2,1)}, u32[]{:S(2)}, u32[]{:S(2)}) async-start(bf16[16,48,2048]{2,1,0:T(8,128)(2,1)} %bitcast.63), calls=%async_computation.1 | async-start | bytes 6291456 | tf_op jit(solution)/shard_map/all_to_all | solution.py:68
  184.6 0.0 copy-start.8
  184.6 4.7 %fusion = f32[768,768]{1,0:T(8,128)S(1)} fusion(bf16[768,2048]{1,0:T(8,128)(2,1)} %bitcast.11, bf16[1,768,2048]{2,1,0:T(8,128)(2,1)S(1)} %copy-done), kind=kOutput, calls=%fused_computation.7 | convolution fusion | flops 2415919104 | bytes 8650752 | tf_op jit(solution)/shard_map/dot_general | solution.py:15
  189.3 0.0 copy-start.6
  189.3 3.3 fusion.6
  192.7 4.1 %add_convert_fusion = bf16[768,2048]{1,0:T(8,128)(2,1)} fusion(f32[768,2048]{1,0:T(8,128)S(1)} %fusion.6, bf16[1,2048,768]{2,1,0:T(8,128)(2,1)S(1)} %copy-done.6, f32[768,768]{1,0:T(8,128)S(1)} %fusion, f32[768,768]{1,0:T(8,128)S(1)} %copy-done.8), kind=kOutput, calls=%fused_computation.5 | convolution fusion | flops 2422603776 | bytes 17301504 | tf_op jit(solution)/shard_map/dot_general | solution.py:25
  196.8 57.7 %all-to-all-done.1 = bf16[16,48,2048]{2,1,0:T(8,128)(2,1)} async-done(((bf16[16,48,2048]{2,1,0:T(8,128)(2,1)}), bf16[16,48,2048]{2,1,0:T(8,128)(2,1)}, u32[]{:S(2)}, u32[]{:S(2)}) %all-to-all-start.1) | async-done | bytes 3145760 | tf_op jit(solution)/shard_map/all_to_all | solution.py:68
  254.6 5.0 %all-to-all-start.3 = ((bf16[16,48,2048]{2,1,0:T(8,128)(2,1)}), bf16[16,48,2048]{2,1,0:T(8,128)(2,1)}, u32[]{:S(2)}, u32[]{:S(2)}) async-start(bf16[16,48,2048]{2,1,0:T(8,128)(2,1)} %bitcast.62), calls=%async_computation.3 | async-start | bytes 6291456 | tf_op jit(solution)/shard_map/all_to_all | solution.py:69
  259.6 0.2 copy.14
  259.8 7.4 %gather_fusion.1 = bf16[384,2048]{1,0:T(8,128)(2,1)} fusion(bf16[768,2048]{1,0:T(8,128)(2,1)} %bitcast.7, s32[1024]{0:T(1024)S(1)} %pad_clamp_fusion), kind=kCustom, calls=%fused_computation.1 | custom fusion | bytes 3147264 | tf_op jit(solution)/shard_map/gather | solution.py:72
  267.2 5.2 %reshape.94 = bf16[128,3,2048]{2,1,0:T(4,128)(2,1)} reshape(bf16[384,2048]{1,0:T(8,128)(2,1)} %gather_fusion.1) | data formatting | bytes 3145728 | tf_op jit(solution)/shard_map/reshape | solution.py:73
  272.3 4.5 %fusion.12 = f32[128,1,3]{2,1,0:T(1,128)S(1)} fusion(bf16[128,3,2048]{2,1,0:T(4,128)(2,1)} %reshape.94, bf16[128,2048,1]{1,0,2:T(8,128)(2,1)} %bitcast.59), kind=kOutput, calls=%fused_computation.27 | convolution fusion | flops 1572864 | bytes 2098688 | tf_op jit(solution)/shard_map/td,tkd->tk/dot_general | solution.py:83
  276.8 0.7 copy.18
  277.5 3.9 %fusion.27 = bf16[128,1,2048]{2,1,0:T(2,128)(2,1)} fusion(bf16[128,3,2048]{2,1,0:T(4,128)(2,1)} %reshape.94, bf16[128,3,1]{1,2,0:T(2,128)(2,1)S(1)} %copy.14), kind=kOutput, calls=%fused_computation.54 | convolution fusion | flops 1572864 | bytes 2097920 | tf_op jit(solution)/shard_map/tk,tkd->td/dot_general | solution.py:81
  281.4 48.2 %all-to-all-done.3 = bf16[16,48,2048]{2,1,0:T(8,128)(2,1)} async-done(((bf16[16,48,2048]{2,1,0:T(8,128)(2,1)}), bf16[16,48,2048]{2,1,0:T(8,128)(2,1)}, u32[]{:S(2)}, u32[]{:S(2)}) %all-to-all-start.3) | async-done | bytes 3145760 | tf_op jit(solution)/shard_map/all_to_all | solution.py:69
  329.6 7.3 %gather_fusion.3 = bf16[384,2048]{1,0:T(8,128)(2,1)} fusion(bf16[768,2048]{1,0:T(8,128)(2,1)} %bitcast.13, s32[1024]{0:T(1024)S(1)} %pad_clamp_fusion), kind=kCustom, calls=%fused_computation.3 | custom fusion | bytes 3147264 | tf_op jit(solution)/shard_map/gather | solution.py:77
  337.0 5.2 %reshape.98 = bf16[128,3,2048]{2,1,0:T(4,128)(2,1)} reshape(bf16[384,2048]{1,0:T(8,128)(2,1)} %gather_fusion.3) | data formatting | bytes 3145728 | tf_op jit(solution)/shard_map/reshape | solution.py:78
  342.1 2.9 fusion.28
  345.0 1.6 bitcast_convert_fusion
  (19 shorter events, 0.1 us)
Async XLA Ops:
  0.6 118.7 %copy-start = (bf16[1,768,2048]{2,1,0:T(8,128)(2,1)S(1)}, bf16[1,768,2048]{2,1,0:T(8,128)(2,1)}, u32[]{:S(2)}) copy-start(bf16[1,768,2048]{2,1,0:T(8,128)(2,1)} %param.13) | copy-start | bytes 9437188
  104.5 75.2 %all-to-all-start.2 = ((bf16[16,48,2048]{2,1,0:T(8,128)(2,1)}), bf16[16,48,2048]{2,1,0:T(8,128)(2,1)}, u32[]{:S(2)}, u32[]{:S(2)}) async-start(bf16[16,48,2048]{2,1,0:T(8,128)(2,1)} %get-tuple-element.3), calls=%async_computation.2 | async-start | bytes 6291456 | tf_op jit(solution)/shard_map/all_to_all | solution.py:58
  109.7 5.6 %copy-start.1 = (bf16[16,48,2048]{2,1,0:T(8,128)(2,1)S(1)}, bf16[16,48,2048]{2,1,0:T(8,128)(2,1)}, u32[]{:S(2)}) copy-start(bf16[16,48,2048]{2,1,0:T(8,128)(2,1)} %all_to_all.20) | copy-start | bytes 9437188
  109.7 5.6 %copy-start.5 = (bf16[1,2048,768]{2,1,0:T(8,128)(2,1)S(1)}, bf16[1,2048,768]{2,1,0:T(8,128)(2,1)}, u32[]{:S(2)}) copy-start(bf16[1,2048,768]{2,1,0:T(8,128)(2,1)} %param.12) | copy-start | bytes 9437188
  115.3 2.6 copy-start.7
  117.9 1.4 copy-start.9
  179.7 74.9 %all-to-all-start.1 = ((bf16[16,48,2048]{2,1,0:T(8,128)(2,1)}), bf16[16,48,2048]{2,1,0:T(8,128)(2,1)}, u32[]{:S(2)}, u32[]{:S(2)}) async-start(bf16[16,48,2048]{2,1,0:T(8,128)(2,1)} %bitcast.63), calls=%async_computation.1 | async-start | bytes 6291456 | tf_op jit(solution)/shard_map/all_to_all | solution.py:68
  184.6 4.7 %copy-start.4 = (bf16[1,2048,768]{2,1,0:T(8,128)(2,1)S(1)}, bf16[1,2048,768]{2,1,0:T(8,128)(2,1)}, u32[]{:S(2)}) copy-start(bf16[1,2048,768]{2,1,0:T(8,128)(2,1)} %param.11) | copy-start | bytes 9437188
  184.6 4.7 %copy-start.8 = (f32[768,768]{1,0:T(8,128)S(1)}, f32[768,768]{1,0:T(8,128)}, u32[]{:S(2)}) copy-start(f32[768,768]{1,0:T(8,128)} %copy-done.7) | copy-start | bytes 7077892
  184.6 4.7 %copy-start.10 = (f32[768,768]{1,0:T(8,128)S(1)}, f32[768,768]{1,0:T(8,128)}, u32[]{:S(2)}) copy-start(f32[768,768]{1,0:T(8,128)} %copy-done.9) | copy-start | bytes 7077892
  189.3 3.4 copy-start.6
  254.6 5.0 %copy-start.3 = (f32[128,3]{0,1:T(4,128)S(1)}, f32[128,3]{0,1:T(4,128)}, u32[]{:S(2)}) copy-start(f32[128,3]{0,1:T(4,128)} %param.10) | copy-start | bytes 4612
  254.6 75.0 %all-to-all-start.3 = ((bf16[16,48,2048]{2,1,0:T(8,128)(2,1)}), bf16[16,48,2048]{2,1,0:T(8,128)(2,1)}, u32[]{:S(2)}, u32[]{:S(2)}) async-start(bf16[16,48,2048]{2,1,0:T(8,128)(2,1)} %bitcast.62), calls=%async_computation.3 | async-start | bytes 6291456 | tf_op jit(solution)/shard_map/all_to_all | solution.py:69
  342.1 2.9 copy-start.2
where the time goes:
time: 347 us
  waiting for transfers between devices  162 us (47%)
  blocking collectives  76.2 us (22%)
  local copies, waits for them, and re-layouts  50.2 us (14%)
  matrix products  35.7 us (10%)
  starting transfers between devices  15.2 us (4%)
  other arithmetic  6.18 us (2%)
    all_to_all x1, blocking collectives, on_device(): lax.all_to_all(send_x, 'expert', split_axis=0, concat_axis=0, tiled=True)  76.2 us
    all_to_all x1, waiting for transfers between devices, on_device(): lax.all_to_all(result_out, 'expert', split_axis=0, concat_axis=0, tiled=T...  57.7 us
    all_to_all x1, waiting for transfers between devices, on_device(): lax.all_to_all(send_g, 'expert', split_axis=0, concat_axis=0, tiled=True)  56.3 us
    all_to_all x1, waiting for transfers between devices, on_device(): lax.all_to_all(result_back, 'expert', split_axis=0, concat_axis=0, tiled=...  48.2 us
    gather x1, local copies, waits for them, and re-layouts, on_device(): tokens[token_of_slot]  8.28 us
    gather x1, local copies, waits for them, and re-layouts, on_device(): cotangent[token_of_slot]  8.24 us
    gather x1, local copies, waits for them, and re-layouts, on_device(): back_out.reshape(total_slots, model_width)[slot_flat]  7.37 us
    gather x1, local copies, waits for them, and re-layouts, on_device(): back_grad.reshape(total_slots, model_width)[slot_flat]  7.34 us
  transfers between devices with their start and end apart: 3, of which 3 were waited for; matrix products, arithmetic and copies ran while one was open for 13% of the time, Pallas kernels for 0%

commit v1 on v0

--- a/solution.py
+++ b/solution.py
@@ -1,7 +1,15 @@
 import jax
 import jax.numpy as jnp
 from jax import lax
+from jax.experimental import pallas as pl
+from jax.experimental.pallas import tpu as pltpu
 from jax.sharding import PartitionSpec as P
+
+PLANE = 4
+LAYERS = 4
+MESH = pl.DeviceIdType.MESH
+ORDER = ((0, 1, 2, 3), (1, 0, 2, 3), (2, 3, 1, 0), (3, 2, 1, 0))
+GRAD_STEP = 2
 
 
 def expert_rows(row_inputs, row_grads, weights):
@@ -84,6 +92,395 @@
     return (mixed, grad_tokens, grad_combine)
 
 
+def nt_dot(a, b):
+    return lax.dot_general(a, b, (((1,), (1,)), ((), ())), preferred_element_type=jnp.float32)
+
+
+def fused_kernel(
+    x_hbm, g_hbm, ids_ref, comb_ref, wg_hbm, wu_hbm, wd_hbm,
+    mixed_ref, grad_ref, gcomb_ref,
+    wg, wu, wd, xg, meta, send_rows, recv_rows, gate_buf, up_buf, ret_rows, part, zrecv,
+    dsend, drecv,
+    w_sem, own_sem, meta_ss, meta_rs, up_ss, down_ss, line_rs, y_ss, y_rs, r_ss, r_rs,
+    p_ss, p_rs, d_ss, d_rs,
+):
+    tok_rows, width = x_hbm.shape
+    fanout = ids_ref.shape[0]
+    cap = send_rows.shape[3]
+    slots = PLANE * cap
+    holders = PLANE * LAYERS
+    me = lax.axis_index("expert")
+    z = me // PLANE
+    p = me % PLANE
+
+    def order(t):
+        power = 1 + 3 * z + 9 * (z * (z - 1) // 2) + 27 * (z * (z - 1) * (z - 2) // 6)
+        code = 0
+        for step in range(LAYERS):
+            packed = sum(ORDER[layer][step] * 4**layer for layer in range(LAYERS))
+            code = code + packed * one_if(t, step)
+        return (code // power) % 4
+
+    def one_if(t, step):
+        d = (t - step) * (t - step)
+        return (10 - d) // 10
+
+    def peer(layer, place):
+        return {"expert": layer * PLANE + place}
+
+    def remote(src, dst, ss, rs, dev):
+        return pltpu.make_async_remote_copy(
+            src_ref=src, dst_ref=dst, send_sem=ss, recv_sem=rs, device_id=dev, device_id_type=MESH
+        )
+
+    w_copies = [
+        pltpu.make_async_copy(wg_hbm.at[0], wg, w_sem.at[0]),
+        pltpu.make_async_copy(wu_hbm.at[0], wu, w_sem.at[1]),
+        pltpu.make_async_copy(wd_hbm.at[0], wd, w_sem.at[2]),
+    ]
+    own_copies = [
+        pltpu.make_async_copy(x_hbm, xg.at[0, z], own_sem.at[0]),
+        pltpu.make_async_copy(g_hbm, xg.at[1, z], own_sem.at[1]),
+    ]
+    for copy in own_copies + w_copies:
+        copy.start()
+
+    barrier = pltpu.get_barrier_semaphore()
+    for o in range(1, LAYERS):
+        pl.semaphore_signal(
+            barrier, inc=1, device_id=peer((z + o) % LAYERS, p), device_id_type=MESH
+        )
+    for o in range(1, PLANE):
+        pl.semaphore_signal(
+            barrier, inc=1, device_id=peer(z, (p + o) % PLANE), device_id_type=MESH
+        )
+
+    experts = lax.broadcasted_iota(jnp.int32, (holders, tok_rows), 0)
+    chosen = jnp.zeros((holders, tok_rows), jnp.float32)
+    weight = jnp.zeros((holders, tok_rows), jnp.float32)
+    for k in range(fanout):
+        hit = ids_ref[k : k + 1, :] == experts
+        chosen = chosen + jnp.where(hit, 1.0, 0.0)
+        weight = weight + jnp.where(hit, comb_ref[k : k + 1, :], 0.0)
+    earlier = lax.broadcasted_iota(jnp.int32, (tok_rows, tok_rows), 0)
+    later = lax.broadcasted_iota(jnp.int32, (tok_rows, tok_rows), 1)
+    before = jnp.where(earlier < later, 1.0, 0.0).astype(jnp.bfloat16)
+    rank = jnp.dot(chosen.astype(jnp.bfloat16), before, preferred_element_type=jnp.float32)
+    rank = jnp.where(chosen > 0.5, rank, -1.0)
+    for layer in range(LAYERS):
+        at = slice(layer * PLANE, (layer + 1) * PLANE)
+        meta[z, layer] = jnp.concatenate([rank[at], weight[at]], axis=0)
+
+    pl.semaphore_wait(barrier, LAYERS + PLANE - 2)
+
+    def meta_copy(o):
+        layer = (z + o) % LAYERS
+        return remote(
+            meta.at[z], meta.at[z], meta_ss.at[layer], meta_rs.at[z], peer(layer, p)
+        )
+
+    def meta_wait(s):
+        remote(meta.at[s], meta.at[s], meta_ss.at[s], meta_rs.at[s], peer(s, p)).wait_recv()
+
+    def up_copy(ph, s):
+        block = xg.at[ph, s]
+        return remote(block, block, up_ss.at[ph, s], line_rs.at[ph, s], peer(z + 1, p))
+
+    def down_copy(ph, s):
+        block = xg.at[ph, s]
+        return remote(block, block, down_ss.at[ph, s], line_rs.at[ph, s], peer(z - 1, p))
+
+    def row_copy(ph, s, q):
+        return remote(
+            send_rows.at[ph, s, q], recv_rows.at[ph, s, p], y_ss.at[ph, s, q],
+            y_rs.at[ph, s, p], peer(z, q),
+        )
+
+    def row_wait(ph, s, q):
+        remote(
+            send_rows.at[ph, s, q], recv_rows.at[ph, s, q], y_ss.at[ph, s, q],
+            y_rs.at[ph, s, q], peer(z, q),
+        ).wait_recv()
+
+    def ret_copy(ph, s, q):
+        return remote(
+            recv_rows.at[ph, s, q], ret_rows.at[ph, s, p], r_ss.at[ph, s, q],
+            r_rs.at[ph, s, p], peer(z, q),
+        )
+
+    def ret_wait(ph, s, q):
+        remote(
+            recv_rows.at[ph, s, q], ret_rows.at[ph, s, q], r_ss.at[ph, s, q],
+            r_rs.at[ph, s, q], peer(z, q),
+        ).wait_recv()
+
+    def part_copy(ph, s):
+        return remote(
+            part.at[ph, s], zrecv.at[ph, z], p_ss.at[ph, s], p_rs.at[ph, z], peer(s, p)
+        )
+
+    def dot_copy(s):
+        return remote(dsend.at[s], drecv.at[z], d_ss.at[s], d_rs.at[z], peer(s, p))
+
+    def forward(ph, s):
+        @pl.when((s <= z) & (z < LAYERS - 1))
+        def _():
+            up_copy(ph, s).start()
+
+        @pl.when((s >= z) & (z > 0))
+        def _():
+            down_copy(ph, s).start()
+
+    own_copies[0].wait()
+    forward(0, z)
+    for o in range(1, LAYERS):
+        meta_copy(o).start()
+    own_copies[1].wait()
+    for copy in w_copies:
+        copy.wait()
+
+    row_id = lax.broadcasted_iota(jnp.int32, (cap, tok_rows), 0).astype(jnp.float32)
+
+    def picks(s):
+        tables = meta[s, z]
+        return [tables[q : q + 1] == row_id for q in range(PLANE)], tables
+
+    def send_stage(i):
+        ph, t = i // LAYERS, i % LAYERS
+        s = order(t)
+
+        @pl.when(t > 0)
+        def _():
+            @pl.when(ph == 0)
+            def _():
+                meta_wait(s)
+
+            remote(
+                xg.at[ph, s], xg.at[ph, s], up_ss.at[ph, s], line_rs.at[ph, s], peer(s, p)
+            ).wait_recv()
+            forward(ph, s)
+
+        @pl.when(i == GRAD_STEP)
+        def _():
+            forward(1, z)
+
+        hits, _ = picks(s)
+        select = jnp.concatenate(
+            [jnp.where(hit, 1.0, 0.0) for hit in hits], axis=0
+        ).astype(jnp.bfloat16)
+        rows = jnp.dot(select, xg[ph, s], preferred_element_type=jnp.float32)
+        send_rows[ph, s] = rows.astype(jnp.bfloat16).reshape(PLANE, cap, width)
+        for o in range(1, PLANE):
+            row_copy(ph, s, (p + o) % PLANE).start()
+        recv_rows[ph, s, p] = send_rows[ph, s, p]
+
+    def expert_stage(i):
+        ph, t = i // LAYERS, i % LAYERS
+        s = order(t)
+        for o in range(1, PLANE):
+            row_wait(ph, s, (p + o) % PLANE)
+
+        @pl.when(ph == 0)
+        def _():
+            rows = recv_rows[0, s].reshape(slots, width)
+            gate = jnp.dot(rows, wg[...], preferred_element_type=jnp.float32)
+            upper = jnp.dot(rows, wu[...], preferred_element_type=jnp.float32)
+            gate_buf[s] = gate
+            up_buf[s] = upper
+            hidden = (gate * jax.nn.sigmoid(gate) * upper).astype(jnp.bfloat16)
+            out = jnp.dot(hidden, wd[...], preferred_element_type=jnp.float32)
+            recv_rows[0, s] = out.astype(jnp.bfloat16).reshape(PLANE, cap, width)
+
+        @pl.when(ph == 1)
+        def _():
+            rows = recv_rows[1, s].reshape(slots, width)
+            d_hidden = nt_dot(rows, wd[...])
+            gate = gate_buf[s]
+            upper = up_buf[s]
+            sig = jax.nn.sigmoid(gate)
+            d_gate = (d_hidden * upper * sig * (1.0 + gate * (1.0 - sig))).astype(jnp.bfloat16)
+            d_upper = (d_hidden * (gate * sig)).astype(jnp.bfloat16)
+            back = nt_dot(d_gate, wg[...]) + nt_dot(d_upper, wu[...])
+            recv_rows[1, s] = back.astype(jnp.bfloat16).reshape(PLANE, cap, width)
+
+        for o in range(1, PLANE):
+            ret_copy(ph, s, (p + o) % PLANE).start()
+        ret_rows[ph, s, p] = recv_rows[ph, s, p]
+
+    def combine_stage(i):
+        ph, t = i // LAYERS, i % LAYERS
+        s = order(t)
+        for o in range(1, PLANE):
+            ret_wait(ph, s, (p + o) % PLANE)
+        hits, tables = picks(s)
+        weights = jnp.concatenate(
+            [
+                jnp.where(hits[q], tables[PLANE + q : PLANE + q + 1], 0.0)
+                for q in range(PLANE)
+            ],
+            axis=0,
+        )
+        high = weights.astype(jnp.bfloat16)
+        low = (weights - high.astype(jnp.float32)).astype(jnp.bfloat16)
+        rows = ret_rows[ph, s].reshape(slots, width)
+        first = (((0,), (0,)), ((), ()))
+        total = lax.dot_general(high, rows, first, preferred_element_type=jnp.float32)
+        total = total + lax.dot_general(low, rows, first, preferred_element_type=jnp.float32)
+        total = total.astype(jnp.bfloat16)
+
+        @pl.when(t == 0)
+        def _():
+            zrecv[ph, z] = total
+
+        @pl.when(t > 0)
+        def _():
+            part[ph, s] = total
+            part_copy(ph, s).start()
+
+        @pl.when(ph == 1)
+        def _():
+            out = ret_rows[0, s].reshape(slots, width)
+            pairs = nt_dot(out, xg[1, s])
+            sums = [
+                jnp.sum(
+                    jnp.where(hits[q], pairs[q * cap : (q + 1) * cap], 0.0), axis=0, keepdims=True
+                )
+                for q in range(PLANE)
+            ]
+            table = jnp.concatenate(sums + [jnp.zeros((8 - PLANE, tok_rows), jnp.float32)], axis=0)
+
+            @pl.when(t == 0)
+            def _():
+                drecv[z] = table
+
+            @pl.when(t > 0)
+            def _():
+                dsend[s] = table
+                dot_copy(s).start()
+
+    items = 2 * LAYERS
+
+    def step(i, carry):
+        @pl.when(i < items)
+        def _():
+            send_stage(i)
+
+        @pl.when((i >= 1) & (i < items + 1))
+        def _():
+            expert_stage(i - 1)
+
+        @pl.when(i >= 2)
+        def _():
+            combine_stage(i - 2)
+
+        return carry
+
+    lax.fori_loop(0, items + 2, step, 0)
+
+    for ph, target in ((0, mixed_ref), (1, grad_ref)):
+        for o in range(1, LAYERS):
+            s = (z + o) % LAYERS
+            remote(
+                part.at[ph, s], zrecv.at[ph, s], p_ss.at[ph, s], p_rs.at[ph, s], peer(s, p)
+            ).wait_recv()
+        total = zrecv[ph, 0].astype(jnp.float32)
+        for s in range(1, LAYERS):
+            total = total + zrecv[ph, s].astype(jnp.float32)
+        target[...] = total.astype(jnp.bfloat16)
+    for o in range(1, LAYERS):
+        s = (z + o) % LAYERS
+        remote(dsend.at[s], drecv.at[s], d_ss.at[s], d_rs.at[s], peer(s, p)).wait_recv()
+    table = jnp.concatenate([drecv[layer, :PLANE] for layer in range(LAYERS)], axis=0)
+    for k in range(fanout):
+        hit = ids_ref[k : k + 1, :] == experts
+        gcomb_ref[k : k + 1, :] = jnp.sum(jnp.where(hit, table, 0.0), axis=0, keepdims=True)
+
+    for o in range(1, LAYERS):
+        s = (z + o) % LAYERS
+        meta_copy(o).wait_send()
+        dot_copy(s).wait_send()
+        for ph in range(2):
+            part_copy(ph, s).wait_send()
+
+    def drain(i, carry):
+        ph, s = i // LAYERS, i % LAYERS
+
+        @pl.when((s <= z) & (z < LAYERS - 1))
+        def _():
+            up_copy(ph, s).wait_send()
+
+        @pl.when((s >= z) & (z > 0))
+        def _():
+            down_copy(ph, s).wait_send()
+
+        for o in range(1, PLANE):
+            row_copy(ph, s, (p + o) % PLANE).wait_send()
+            ret_copy(ph, s, (p + o) % PLANE).wait_send()
+        return carry
+
+    lax.fori_loop(0, items, drain, 0)
+
+
+def fused_on_device(tokens, cotangent, expert_ids, combine, w_gate, w_up, w_down):
+    holders = lax.axis_size("expert")
+    tok_rows, width = tokens.shape
+    fanout = expert_ids.shape[1]
+    cap = 2 * tok_rows * fanout // holders
+    inner = w_gate.shape[2]
+    slots = PLANE * cap
+    bf, f32 = jnp.bfloat16, jnp.float32
+    hbm = pl.BlockSpec(memory_space=pl.ANY)
+    vmem = pl.BlockSpec(memory_space=pltpu.VMEM)
+    dma = pltpu.SemaphoreType.DMA
+    rows = pltpu.VMEM((2, LAYERS, PLANE, cap, width), bf)
+    blocks = pltpu.VMEM((2, LAYERS, tok_rows, width), bf)
+    mixed, grad_tokens, gcomb = pl.pallas_call(
+        fused_kernel,
+        out_shape=(
+            jax.ShapeDtypeStruct((tok_rows, width), bf),
+            jax.ShapeDtypeStruct((tok_rows, width), bf),
+            jax.ShapeDtypeStruct((fanout, tok_rows), f32),
+        ),
+        in_specs=[hbm, hbm, vmem, vmem, hbm, hbm, hbm],
+        out_specs=(vmem, vmem, vmem),
+        scratch_shapes=[
+            pltpu.VMEM(w_gate.shape[1:], bf),
+            pltpu.VMEM(w_up.shape[1:], bf),
+            pltpu.VMEM(w_down.shape[1:], bf),
+            blocks,
+            pltpu.VMEM((LAYERS, LAYERS, 2 * PLANE, tok_rows), f32),
+            rows,
+            rows,
+            pltpu.VMEM((LAYERS, slots, inner), f32),
+            pltpu.VMEM((LAYERS, slots, inner), f32),
+            rows,
+            blocks,
+            blocks,
+            pltpu.VMEM((LAYERS, 8, tok_rows), f32),
+            pltpu.VMEM((LAYERS, 8, tok_rows), f32),
+            dma((3,)),
+            dma((2,)),
+            dma((LAYERS,)),
+            dma((LAYERS,)),
+            dma((2, LAYERS)),
+            dma((2, LAYERS)),
+            dma((2, LAYERS)),
+            dma((2, LAYERS, PLANE)),
+            dma((2, LAYERS, PLANE)),
+            dma((2, LAYERS, PLANE)),
+            dma((2, LAYERS, PLANE)),
+            dma((2, LAYERS)),
+            dma((2, LAYERS)),
+            dma((LAYERS,)),
+            dma((LAYERS,)),
+        ],
+        compiler_params=pltpu.CompilerParams(
+            collective_id=0, has_side_effects=True, vmem_limit_bytes=60 * 2**20
+        ),
+    )(tokens, cotangent, expert_ids.T, combine.T, w_gate, w_up, w_down)
+    return mixed, grad_tokens, gcomb.T
+
+
 def solution(mesh):
     placed = (
         P(("groups", "expert"), None),
@@ -94,8 +491,9 @@
         P("expert", None, None),
         P("expert", None, None),
     )
+    fits = mesh.shape["expert"] == PLANE * LAYERS
     return jax.shard_map(
-        on_device,
+        fused_on_device if fits else on_device,
         mesh=mesh,
         in_specs=placed,
         out_specs=(

time: 347 us -> 195 us (0.56)
  the two profiles are of different devices: /device:TPU:13 before, /device:TPU:1 now
where the time goes in v1:
time: 195 us
  Pallas kernels  189 us (97%)
  local copies, waits for them, and re-layouts  5.02 us (3%)
    pallas_call x1, Pallas kernels, fused_on_device(): pl.pallas_call(fused_kernel, out_shape=(jax.ShapeDtypeStruct((tok_rows, w...  189 us
    unnamed x3, local copies, waits for them, and re-layouts  5.02 us

profile of v1, /device:TPU:1, one launch (start us, length us, event | category | flops | bytes accessed | tf_op | source)
XLA Modules:
  0.0 195.0 jit_solution(4710187325267431508)
XLA Ops:
  0.6 189.3 %shard_map.94 = (bf16[128,2048]{1,0:T(8,128)(2,1)}, bf16[128,2048]{1,0:T(8,128)(2,1)}, f32[3,128]{1,0:T(4,128)}) custom-call(bf16[128,2048]{1,0:T(8,128)(2,1)} %x_hbm.1, bf16[128,2048]{1,0:T(8,128)(2,1)} %g_hbm.1, s32[3,128]{1,0:T(4,128)} %bitcast.3, f32[3,128]{1,0:T(4,128)} %bitcast.4, bf16[1,2048,768]{2,1,0:T(8,128)(2,1)} %wg_hbm.1, ...), custom_call_target="tpu_custom_call" | custom-call | tf_op jit(solution)/shard_map/pallas_call | solution.py:437
  190.0 1.9 copy.13
  191.9 1.9 copy.14
  193.7 1.3 copy.15

commit v2 on v1

--- a/solution.py
+++ b/solution.py
@@ -1,3 +1,5 @@
+import functools
+
 import jax
 import jax.numpy as jnp
 from jax import lax
@@ -8,8 +10,18 @@
 PLANE = 4
 LAYERS = 4
 MESH = pl.DeviceIdType.MESH
+CHAINED = 1
+SCHEDULE = (
+    ("line", 0),
+    ("grad", 4),
+    ("send", 0),
+    ("weight", 1),
+    ("expert", 1),
+    ("combine", 2),
+    ("relay", 3),
+    ("chain", 5),
+)
 ORDER = ((0, 1, 2, 3), (1, 0, 2, 3), (2, 3, 1, 0), (3, 2, 1, 0))
-GRAD_STEP = 2
 
 
 def expert_rows(row_inputs, row_grads, weights):
@@ -99,10 +111,10 @@
 def fused_kernel(
     x_hbm, g_hbm, ids_ref, comb_ref, wg_hbm, wu_hbm, wd_hbm,
     mixed_ref, grad_ref, gcomb_ref,
-    wg, wu, wd, xg, meta, send_rows, recv_rows, gate_buf, up_buf, ret_rows, part, zrecv,
+    wg, wu, wd, xg, meta, send_rows, recv_rows, gate_buf, up_buf, ret_rows, part, zrecv, relay, chain,
     dsend, drecv,
     w_sem, own_sem, meta_ss, meta_rs, up_ss, down_ss, line_rs, y_ss, y_rs, r_ss, r_rs,
-    p_ss, p_rs, d_ss, d_rs,
+    p_ss, p_rs, d_ss, d_rs, relay_rs, chain_rs,
 ):
     tok_rows, width = x_hbm.shape
     fanout = ids_ref.shape[0]
@@ -120,6 +132,10 @@
             packed = sum(ORDER[layer][step] * 4**layer for layer in range(LAYERS))
             code = code + packed * one_if(t, step)
         return (code // power) % 4
+
+    def item(i):
+        first = (i // 2 + 2) // 3
+        return (1 - first) * i + first * ((i + 1) // 6), first * ((i + 1) % 3 + 1)
 
     def one_if(t, step):
         d = (t - step) * (t - step)
@@ -214,9 +230,30 @@
             r_rs.at[ph, s, q], peer(z, q),
         ).wait_recv()
 
+    mate = z + 1 - 2 * (z % 2)
+    inner = (z >= 1) & (z <= LAYERS - 2)
+    outer = (z < 1) | (z > LAYERS - 2)
+    other_inner = 2 - z // 2
+
     def part_copy(ph, s):
         return remote(
             part.at[ph, s], zrecv.at[ph, z], p_ss.at[ph, s], p_rs.at[ph, z], peer(s, p)
+        )
+
+    def part_wait(ph, s):
+        remote(
+            part.at[ph, s], zrecv.at[ph, s], p_ss.at[ph, s], p_rs.at[ph, s], peer(s, p)
+        ).wait_recv()
+
+    def chain_copy(ph, s):
+        return remote(
+            part.at[ph, s], chain.at[ph], p_ss.at[ph, s], chain_rs.at[ph], peer(other_inner, p)
+        )
+
+    def relay_copy(ph, s):
+        return remote(
+            part.at[ph, s], relay.at[ph, s % 2], p_ss.at[ph, s], relay_rs.at[ph, s % 2],
+            peer(mate, p),
         )
 
     def dot_copy(s):
@@ -236,8 +273,6 @@
     for o in range(1, LAYERS):
         meta_copy(o).start()
     own_copies[1].wait()
-    for copy in w_copies:
-        copy.wait()
 
     row_id = lax.broadcasted_iota(jnp.int32, (cap, tok_rows), 0).astype(jnp.float32)
 
@@ -245,8 +280,8 @@
         tables = meta[s, z]
         return [tables[q : q + 1] == row_id for q in range(PLANE)], tables
 
-    def send_stage(i):
-        ph, t = i // LAYERS, i % LAYERS
+    def line_stage(i):
+        ph, t = item(i)
         s = order(t)
 
         @pl.when(t > 0)
@@ -260,9 +295,9 @@
             ).wait_recv()
             forward(ph, s)
 
-        @pl.when(i == GRAD_STEP)
-        def _():
-            forward(1, z)
+    def send_stage(i):
+        ph, t = item(i)
+        s = order(t)
 
         hits, _ = picks(s)
         select = jnp.concatenate(
@@ -275,7 +310,7 @@
         recv_rows[ph, s, p] = send_rows[ph, s, p]
 
     def expert_stage(i):
-        ph, t = i // LAYERS, i % LAYERS
+        ph, t = item(i)
         s = order(t)
         for o in range(1, PLANE):
             row_wait(ph, s, (p + o) % PLANE)
@@ -308,7 +343,7 @@
         ret_rows[ph, s, p] = recv_rows[ph, s, p]
 
     def combine_stage(i):
-        ph, t = i // LAYERS, i % LAYERS
+        ph, t = item(i)
         s = order(t)
         for o in range(1, PLANE):
             ret_wait(ph, s, (p + o) % PLANE)
@@ -335,7 +370,14 @@
         @pl.when(t > 0)
         def _():
             part[ph, s] = total
+
+        @pl.when((t == 1) & (outer | (ph >= CHAINED)))
+        def _():
             part_copy(ph, s).start()
+
+        @pl.when((t > 1) & outer)
+        def _():
+            relay_copy(ph, s).start()
 
         @pl.when(ph == 1)
         def _():
@@ -358,35 +400,84 @@
                 dsend[s] = table
                 dot_copy(s).start()
 
+    def relay_stage(i):
+        ph, t = item(i)
+        s = order(t)
+
+        @pl.when((t > 1) & inner)
+        def _():
+            relay_copy(ph, s).wait_recv()
+            total = part[ph, s].astype(jnp.float32) + relay[ph, s % 2].astype(jnp.float32)
+            part[ph, s] = total.astype(jnp.bfloat16)
+
+            @pl.when((t < LAYERS - 1) | (ph >= CHAINED))
+            def _():
+                part_copy(ph, s).start()
+
+            @pl.when((t == LAYERS - 1) & (ph < CHAINED))
+            def _():
+                chain_copy(ph, s).start()
+
+    def chain_stage(i):
+        ph, t = item(i)
+
+        @pl.when((t == LAYERS - 1) & (ph < CHAINED) & inner)
+        def _():
+            chain_copy(ph, mate).wait_recv()
+            total = part[ph, mate].astype(jnp.float32) + chain[ph].astype(jnp.float32)
+            part[ph, mate] = total.astype(jnp.bfloat16)
+            part_copy(ph, mate).start()
+
     items = 2 * LAYERS
 
+    def grad_stage(i):
+        @pl.when(i == 0)
+        def _():
+            forward(1, z)
+
+    def weight_stage(i):
+        @pl.when(i == 0)
+        def _():
+            for copy in w_copies:
+                copy.wait()
+
+    stages = {
+        "line": line_stage,
+        "grad": grad_stage,
+        "send": send_stage,
+        "weight": weight_stage,
+        "expert": expert_stage,
+        "combine": combine_stage,
+        "relay": relay_stage,
+        "chain": chain_stage,
+    }
+    last = items + max(lag for _, lag in SCHEDULE)
+
     def step(i, carry):
-        @pl.when(i < items)
-        def _():
-            send_stage(i)
-
-        @pl.when((i >= 1) & (i < items + 1))
-        def _():
-            expert_stage(i - 1)
-
-        @pl.when(i >= 2)
-        def _():
-            combine_stage(i - 2)
-
+        for name, lag in SCHEDULE:
+            pl.when((i >= lag) & (i < items + lag))(functools.partial(stages[name], i - lag))
         return carry
 
-    lax.fori_loop(0, items + 2, step, 0)
+    lax.fori_loop(0, last, step, 0)
 
     for ph, target in ((0, mixed_ref), (1, grad_ref)):
-        for o in range(1, LAYERS):
-            s = (z + o) % LAYERS
-            remote(
-                part.at[ph, s], zrecv.at[ph, s], p_ss.at[ph, s], p_rs.at[ph, s], peer(s, p)
-            ).wait_recv()
-        total = zrecv[ph, 0].astype(jnp.float32)
-        for s in range(1, LAYERS):
-            total = total + zrecv[ph, s].astype(jnp.float32)
-        target[...] = total.astype(jnp.bfloat16)
+        part_wait(ph, mate)
+        total = zrecv[ph, z].astype(jnp.float32) + zrecv[ph, mate].astype(jnp.float32)
+
+        def add_other(target=target, ph=ph, total=total):
+            part_wait(ph, other_inner)
+            wide = total + zrecv[ph, other_inner].astype(jnp.float32)
+            target[...] = wide.astype(jnp.bfloat16)
+
+        if ph < CHAINED:
+
+            @pl.when(outer)
+            def _():
+                target[...] = total.astype(jnp.bfloat16)
+
+            pl.when(inner)(add_other)
+        else:
+            add_other()
     for o in range(1, LAYERS):
         s = (z + o) % LAYERS
         remote(dsend.at[s], drecv.at[s], d_ss.at[s], d_rs.at[s], peer(s, p)).wait_recv()
@@ -456,6 +547,8 @@
             rows,
             blocks,
             blocks,
+            pltpu.VMEM((2, 2, tok_rows, width), bf),
+            pltpu.VMEM((2, tok_rows, width), bf),
             pltpu.VMEM((LAYERS, 8, tok_rows), f32),
             pltpu.VMEM((LAYERS, 8, tok_rows), f32),
             dma((3,)),
@@ -473,6 +566,8 @@
             dma((2, LAYERS)),
             dma((LAYERS,)),
             dma((LAYERS,)),
+            dma((2, 2)),
+            dma((2,)),
         ],
         compiler_params=pltpu.CompilerParams(
             collective_id=0, has_side_effects=True, vmem_limit_bytes=60 * 2**20

time: 195 us -> 178 us (0.913)
  Pallas kernels: 189 us -> 172 us
    pallas_call x1, Pallas kernels: 189 us -> 172 us  [fused_on_device(): pl.pallas_call(fused_kernel, out_shape=(jax.ShapeDtypeStruct((tok_rows, w...]
where the time goes in v2:
time: 178 us; the launch traced here: 177 us
  Pallas kernels  172 us (97%)
  local copies, waits for them, and re-layouts  5.02 us (3%)
    pallas_call x1, Pallas kernels, fused_on_device(): pl.pallas_call(fused_kernel, out_shape=(jax.ShapeDtypeStruct((tok_rows, w...  172 us
    unnamed x3, local copies, waits for them, and re-layouts  5.02 us

profile of v2, /device:TPU:1, one launch (start us, length us, event | category | flops | bytes accessed | tf_op | source)
XLA Modules:
  0.0 177.3 jit_solution(9612091829019539155)
XLA Ops:
  0.6 171.7 %shard_map.94 = (bf16[128,2048]{1,0:T(8,128)(2,1)}, bf16[128,2048]{1,0:T(8,128)(2,1)}, f32[3,128]{1,0:T(4,128)}) custom-call(bf16[128,2048]{1,0:T(8,128)(2,1)} %x_hbm.1, bf16[128,2048]{1,0:T(8,128)(2,1)} %g_hbm.1, s32[3,128]{1,0:T(4,128)} %bitcast.3, f32[3,128]{1,0:T(4,128)} %bitcast.4, bf16[1,2048,768]{2,1,0:T(8,128)(2,1)} %wg_hbm.1, ...), custom_call_target="tpu_custom_call" | custom-call | tf_op jit(solution)/shard_map/pallas_call | solution.py:528
  172.3 1.9 %copy.13 = bf16[128,2048]{1,0:T(8,128)(2,1)} copy(bf16[128,2048]{1,0:T(8,128)(2,1)} %get-tuple-element.12) | data formatting | bytes 1048576
  174.2 1.9 %copy.14 = bf16[128,2048]{1,0:T(8,128)(2,1)} copy(bf16[128,2048]{1,0:T(8,128)(2,1)} %get-tuple-element.13) | data formatting | bytes 1048576
  176.1 1.3 copy.15

commit v3 on v2

--- a/solution.py
+++ b/solution.py
@@ -158,7 +158,7 @@
         pltpu.make_async_copy(x_hbm, xg.at[0, z], own_sem.at[0]),
         pltpu.make_async_copy(g_hbm, xg.at[1, z], own_sem.at[1]),
     ]
-    for copy in own_copies + w_copies:
+    for copy in own_copies:
         copy.start()
 
     barrier = pltpu.get_barrier_semaphore()
@@ -272,6 +272,8 @@
     forward(0, z)
     for o in range(1, LAYERS):
         meta_copy(o).start()
+    for copy in w_copies:
+        copy.start()
     own_copies[1].wait()
 
     row_id = lax.broadcasted_iota(jnp.int32, (cap, tok_rows), 0).astype(jnp.float32)

time: 178 us -> 176 us (0.989)
  Pallas kernels: 172 us -> 170 us
    pallas_call x1, Pallas kernels: 172 us -> 170 us  [fused_on_device(): pl.pallas_call(fused_kernel, out_shape=(jax.ShapeDtypeStruct((tok_rows, w...]
where the time goes in v3:
time: 176 us; the launch traced here: 175 us
  Pallas kernels  170 us (97%)
  local copies, waits for them, and re-layouts  5.02 us (3%)
    pallas_call x1, Pallas kernels, fused_on_device(): pl.pallas_call(fused_kernel, out_shape=(jax.ShapeDtypeStruct((tok_rows, w...  170 us
    unnamed x3, local copies, waits for them, and re-layouts  5.02 us

profile of v3, /device:TPU:1, one launch (start us, length us, event | category | flops | bytes accessed | tf_op | source)
XLA Modules:
  0.0 175.4 jit_solution(2211890972832724695)
XLA Ops:
  0.6 169.7 %shard_map.94 = (bf16[128,2048]{1,0:T(8,128)(2,1)}, bf16[128,2048]{1,0:T(8,128)(2,1)}, f32[3,128]{1,0:T(4,128)}) custom-call(bf16[128,2048]{1,0:T(8,128)(2,1)} %x_hbm.1, bf16[128,2048]{1,0:T(8,128)(2,1)} %g_hbm.1, s32[3,128]{1,0:T(4,128)} %bitcast.3, f32[3,128]{1,0:T(4,128)} %bitcast.4, bf16[1,2048,768]{2,1,0:T(8,128)(2,1)} %wg_hbm.1, ...), custom_call_target="tpu_custom_call" | custom-call | tf_op jit(solution)/shard_map/pallas_call | solution.py:530
  170.4 1.9 %copy.13 = bf16[128,2048]{1,0:T(8,128)(2,1)} copy(bf16[128,2048]{1,0:T(8,128)(2,1)} %get-tuple-element.12) | data formatting | bytes 1048576
  172.3 1.9 %copy.14 = bf16[128,2048]{1,0:T(8,128)(2,1)} copy(bf16[128,2048]{1,0:T(8,128)(2,1)} %get-tuple-element.13) | data formatting | bytes 1048576
  174.1 1.3 copy.15
